TPU v7x, 512 devices: a whole 4x8x8 slice. The times are simulated.
512 devices in a mesh: ctx: 16 (over y, core), resp: 8 (over x, z_lo), head: 4 (over z_hi).
Axes of the slice: x: 4, y: 8, z: 8 (z_hi: 4, z_lo: 2; z = z_hi * 2 + z_lo), core: 2. Of those that a mesh axis runs over, the one named last changes fastest.
Arguments:
- queries: bfloat16 [32768, 64, 128], P(('ctx', 'resp'), 'head'), may hold values from -6 to 6, as said below
- prompt_k: bfloat16 [1536, 8, 128], P(('ctx', 'resp'), 'head'), may hold values from -6 to 6, as said below
- prompt_v: bfloat16 [1536, 8, 128], P(('ctx', 'resp'), 'head'), may hold values from -6 to 6
- resp_k: bfloat16 [32768, 8, 128], P(('ctx', 'resp'), 'head'), may hold values from -6 to 6
- resp_v: bfloat16 [32768, 8, 128], P(('ctx', 'resp'), 'head'), may hold values from -6 to 6
- prefix_k: bfloat16 [64, 8, 128], P(None, 'head'), may hold values from -6 to 6
- prefix_v: bfloat16 [64, 8, 128], P(None, 'head'), may hold values from -6 to 6
- d_out: bfloat16 [32768, 64, 128], P(('ctx', 'resp'), 'head'), may hold values from -6 to 6
- shard_mask: int32 [128, 128], P(('ctx', 'resp')), may hold values from 0 to 1, as said below
- resp_lengths: int32 [128], P(('ctx', 'resp')), may hold values from 1 to 256, 16512 in all
- prefix_count: int32 [1], replicated, may hold values from 32 to 64
Outputs:
- attn_out: bfloat16 [32768, 64, 128], P(('ctx', 'resp'), 'head')
- grad_prefix_k: float32 [64, 8, 128], P(None, 'head')
- grad_prefix_v: float32 [64, 8, 128], P(None, 'head')
Inputs may be any that keep to these rules, and one draw needn't show every extreme that they name: `queries`: of order one; rows may be strongly aligned with one another. `prompt_k`: of order one; rows may be strongly aligned with one another. `resp_lengths`: the lengths sum to 16512 and the largest is exactly 256. `shard_mask`: each response attends to a window of 64 consecutive prompt blocks (block-sparse sliding-window prompt attention, no wrap) and no other.
All inputs are finite; a program needn't handle non-finite values. No bound on the sum of `resp_lengths` on one device may be relied on, other than what follows from the above.
Results may differ from a plain program's by a relative error of at most 0.013.
Values may be sent and summed in bfloat16 or wider, within the bound.
A program may use at most 128 MiB of HBM per device.

v0:
```python
import jax
import jax.numpy as jnp
from jax import lax
from jax.sharding import PartitionSpec as P

RLEN = 256
PROMPT_DEV = 12


def prompt_visible(shard_rows, block_start, block_size):
    owners = (block_start + jnp.arange(block_size, dtype=jnp.int32)) // PROMPT_DEV
    onehot = (owners[:, None] == jnp.arange(shard_rows.shape[1], dtype=jnp.int32)[None, :]).astype(
        jnp.float32
    )
    seen_rows = jnp.dot(
        shard_rows.astype(jnp.float32), onehot.T, preferred_element_type=jnp.float32
    )
    seen_rows = jnp.broadcast_to(seen_rows[:, None, :], (seen_rows.shape[0], RLEN, block_size))
    return seen_rows.reshape(-1, block_size) > 0.5


def prompt_scores(grouped, key_block, visible, score_scale):
    scores = (
        jnp.einsum("rgqd,kgd->rgqk", grouped, key_block, preferred_element_type=jnp.float32)
        * score_scale
    )
    return jnp.where(visible[:, None, None, :], scores, -jnp.inf)


def add_stats(stat_pair, scores):
    row_max, row_total = stat_pair
    new_max = jnp.maximum(row_max, jnp.max(scores, axis=-1))
    row_total = row_total * jnp.exp(row_max - new_max) + jnp.sum(
        jnp.exp(scores - new_max[..., None]), axis=-1
    )
    return (new_max, row_total)


def add_values(accumulated, scores, value_block, row_max, row_total):
    weights = (jnp.exp(scores - row_max[..., None]) / row_total[..., None]).astype(jnp.bfloat16)
    return accumulated + jnp.einsum(
        "rgqk,kgd->rgqd", weights, value_block, preferred_element_type=jnp.float32
    )


def per_device(
    queries,
    prompt_k,
    prompt_v,
    resp_k,
    resp_v,
    prefix_k,
    prefix_v,
    d_out,
    shard_mask,
    resp_lengths,
    prefix_count,
):
    tok_rows, head_count, head_width = queries.shape
    kv_local = prompt_k.shape[1]
    q_group = head_count // kv_local
    resp_count = tok_rows // RLEN
    score_scale = head_width ** (-0.5)
    highest = lax.Precision.HIGHEST
    grouped = queries.reshape(tok_rows, kv_local, q_group, head_width)
    prefix_slots = prefix_k.shape[0]
    live_slots = jnp.arange(prefix_slots, dtype=jnp.int32) < prefix_count[0]
    pre_scores = (
        jnp.einsum("rgqd,jgd->rgqj", grouped, prefix_k, preferred_element_type=jnp.float32)
        * score_scale
    )
    pre_scores = jnp.where(live_slots[None, None, None, :], pre_scores, -jnp.inf)
    positions = jnp.arange(RLEN, dtype=jnp.int32)
    per_resp = grouped.reshape(resp_count, RLEN, kv_local, q_group, head_width)
    own_keys = resp_k.reshape(resp_count, RLEN, kv_local, head_width)
    own_values = resp_v.reshape(resp_count, RLEN, kv_local, head_width)
    own_scores = (
        jnp.einsum("brgqd,bkgd->brgqk", per_resp, own_keys, preferred_element_type=jnp.float32)
        * score_scale
    )
    causal = (positions[None, None, :] <= positions[None, :, None]) & (
        positions[None, None, :] < resp_lengths[:, None, None]
    )
    own_scores = jnp.where(causal[:, :, None, None, :], own_scores, -jnp.inf)
    row_max = jnp.maximum(
        jnp.max(pre_scores, axis=-1),
        jnp.max(own_scores, axis=-1).reshape(tok_rows, kv_local, q_group),
    )
    row_total = jnp.sum(jnp.exp(pre_scores - row_max[..., None]), axis=-1)
    row_total = row_total + jnp.sum(
        jnp.exp(own_scores - row_max.reshape(resp_count, RLEN, kv_local, q_group)[..., None]),
        axis=-1,
    ).reshape(tok_rows, kv_local, q_group)
    stat_pair = (row_max, row_total)
    empty = jnp.zeros((tok_rows, kv_local, q_group, head_width), jnp.float32)
    whole_k, whole_v = (
        lax.all_gather(prompt_k, ("ctx", "resp"), axis=0, tiled=True),
        lax.all_gather(prompt_v, ("ctx", "resp"), axis=0, tiled=True),
    )
    prompt_total = whole_k.shape[0]
    for block_start in range(0, prompt_total, 512):
        block_size = min(512, prompt_total - block_start)
        visible = prompt_visible(shard_mask, block_start, block_size)
        key_block = whole_k[block_start : block_start + block_size]

        def stat_step(carried, key_block=key_block, visible=visible):
            return add_stats(carried, prompt_scores(grouped, key_block, visible, score_scale))

        stat_pair = stat_step(stat_pair)
    final_max, final_total = stat_pair
    accumulated = empty
    accumulated = add_values(accumulated, pre_scores, prefix_v, final_max, final_total)
    weights = (
        jnp.exp(own_scores - final_max.reshape(resp_count, RLEN, kv_local, q_group)[..., None])
        / final_total.reshape(resp_count, RLEN, kv_local, q_group)[..., None]
    ).astype(jnp.bfloat16)
    own_mixed = jnp.einsum(
        "brgqk,bkgd->brgqd", weights, own_values, preferred_element_type=jnp.float32
    )
    mixed = accumulated + own_mixed.reshape(tok_rows, kv_local, q_group, head_width)
    for block_start in range(0, prompt_total, 512):
        block_size = min(512, prompt_total - block_start)
        visible = prompt_visible(shard_mask, block_start, block_size)
        key_block = whole_k[block_start : block_start + block_size]
        value_block = whole_v[block_start : block_start + block_size]

        def value_step(carried, key_block=key_block, value_block=value_block, visible=visible):
            scores = prompt_scores(grouped, key_block, visible, score_scale)
            return add_values(carried, scores, value_block, final_max, final_total)

        mixed = value_step(mixed)
    attn_out = mixed.reshape(tok_rows, head_count, head_width).astype(jnp.bfloat16)
    valid_rows = (positions[None, :] < resp_lengths[:, None]).reshape(tok_rows)
    grad_half = jnp.where(valid_rows[:, None, None], d_out, jnp.zeros_like(d_out)).reshape(
        tok_rows, kv_local, q_group, head_width
    )
    grad_rows = grad_half.astype(jnp.float32)
    inner_dot = jnp.sum(grad_rows * mixed, axis=-1)
    exact_pre = jnp.exp(pre_scores - final_max[..., None]) / final_total[..., None]
    d_pre = jnp.einsum("rgqd,jgd->rgqj", grad_half, prefix_v, preferred_element_type=jnp.float32)
    d_scores = exact_pre * (d_pre - inner_dot[..., None])
    grad_v = jnp.einsum("rgqj,rgqd->jgd", exact_pre, grad_rows, precision=highest)
    grad_k = (
        jnp.einsum("rgqj,rgqd->jgd", d_scores, grouped.astype(jnp.float32), precision=highest)
        * score_scale
    )
    grad_k, grad_v = lax.psum((grad_k, grad_v), ("ctx", "resp"))
    return (attn_out, grad_k, grad_v)


def solution(mesh):
    in_specs = (
        P(("ctx", "resp"), "head", None),
        P(("ctx", "resp"), "head", None),
        P(("ctx", "resp"), "head", None),
        P(("ctx", "resp"), "head", None),
        P(("ctx", "resp"), "head", None),
        P(None, "head", None),
        P(None, "head", None),
        P(("ctx", "resp"), "head", None),
        P(("ctx", "resp"), None),
        P(("ctx", "resp")),
        P(),
    )
    out_specs = (P(("ctx", "resp"), "head", None), P(None, "head", None), P(None, "head", None))
    return jax.shard_map(
        per_device, mesh=mesh, in_specs=in_specs, out_specs=out_specs, check_vma=False
    )
```

profile of v0, /device:TPU:1, one launch (start us, length us, event | category | flops | bytes accessed | tf_op | source)
XLA Modules:
  0.0 1582.3 jit_solution(10637793449177359590)
XLA Ops:
  8.1 2.0 fusion.82
  10.1 2.0 broadcast_select_fusion
  12.0 272.6 %all_gather.6 = bf16[1536,2,128]{2,1,0:T(2,128)(2,1)S(1)} all-gather(bf16[12,2,128]{2,1,0:T(2,128)(2,1)} %param.12), channel_id=1, replica_groups=mesh['ctx'=16,'resp'=8,'head'=4] {'ctx','resp'}, dimensions={0}, use_global_device_ids=true | all-gather | bytes 792576 | tf_op jit(solution)/shard_map/all_gather | solution.py:97
  284.6 0.5 fusion.78
  285.1 0.9 fusion.48
  286.0 0.9 fusion.47
  287.0 0.9 fusion.46
  288.6 1.4 bitcast_reduce_fusion
  290.0 1.4 bitcast_reduce_fusion.1
  291.4 1.4 bitcast_reduce_fusion.2
  292.8 0.9 fusion.17
  294.2 0.9 exponential_reduce_fusion
  295.3 2.1 fusion.11
  297.5 0.7 copy-done.3
  298.2 3.9 fusion.2
  302.2 1.5 convolution_bitcast_fusion.1
  303.7 2.7 fusion.21
  306.4 277.0 %all_gather.7 = bf16[1536,2,128]{2,1,0:T(2,128)(2,1)S(1)} all-gather(bf16[12,2,128]{2,1,0:T(2,128)(2,1)S(1)} %copy-done.8), channel_id=1, replica_groups=mesh['ctx'=16,'resp'=8,'head'=4] {'ctx','resp'}, dimensions={0}, use_global_device_ids=true | all-gather | bytes 792576 | tf_op jit(solution)/shard_map/all_gather | solution.py:98
  583.4 1.3 fusion.77
  584.8 1.8 copy.91
  586.6 7.1 fusion.13
  593.7 1.8 copy.92
  595.5 7.2 fusion.15
  602.7 0.9 copy.93
  603.6 7.1 fusion.12
  610.7 1.6 copy.54
  612.3 4.9 multiply_reduce_fusion
  617.5 1.4 fusion.29
  619.0 1.8 copy.57
  620.8 951.7 %all-reduce.3.cloned.1.call-done = (f32[64,2,128]{2,0,1:T(8,128)}, f32[64,2,128]{2,0,1:T(8,128)}) async-done(((f32[64,2,128]{2,0,1:T(8,128)}, f32[64,2,128]{2,0,1:T(8,128)}), (f32[64,2,128]{2,0,1:T(8,128)}, f32[64,2,128]{2,0,1:T(8,128)})) %all-reduce.3.cloned.1.call-update) | async-done | bytes 131088 | tf_op jit(solution)/shard_map/psum | solution.py:147
  1572.4 1.5 copy.58
  1574.0 1.5 copy.59
  (35 shorter events, 1.4 us)
Async XLA Ops:
  7.2 281.4 %copy-start = (bf16[256,16,128]{2,1,0:T(8,128)(2,1)S(1)}, bf16[256,16,128]{2,1,0:T(8,128)(2,1)}, u32[]{:S(2)}) copy-start(bf16[256,16,128]{2,1,0:T(8,128)(2,1)} %param.11) | copy-start | bytes 3145732
  7.2 1565.3 %all-reduce.3.cloned.1.call-start = ((), (), s32[]{:S(2)}) async-start(), calls=%async_computation | async-start | bytes 262144 | tf_op jit(solution)/shard_map/psum | solution.py:147
  290.0 5.3 copy-start.1
  290.0 2.8 copy-start.5
  291.4 6.1 copy-start.2
  291.4 2.3 copy-start.6
  292.8 5.4 copy-start.3
  298.2 5.5 copy-start.9
  303.7 2.7 copy-start.8
  603.6 8.7 copy-start.7
  612.3 4.9 copy-start.4
Sparse Core Ops, SparseCore 0:
  619.1 953.3 all-reduce.2
where the time goes:
time: 1580 us
  waiting for transfers between devices  952 us (60%)
  blocking collectives  550 us (35%)
  matrix products  40.6 us (3%)
    psum x1, waiting for transfers between devices, per_device(): grad_k, grad_v = lax.psum((grad_k, grad_v), ('ctx', 'resp'))  952 us
    all_gather x1, blocking collectives, per_device(): lax.all_gather(prompt_v, ('ctx', 'resp'), axis=0, tiled=True)  277 us
    all_gather x1, blocking collectives, per_device(): lax.all_gather(prompt_k, ('ctx', 'resp'), axis=0, tiled=True)  273 us
  transfers between devices with their start and end apart: 1, of which 1 were waited for; matrix products, arithmetic and copies ran while one was open for 0% of the time, Pallas kernels for 0%

commit v1 on v0

v1 whole, which is shorter than its diff:
```python
import functools
import math

import jax
import jax.numpy as jnp
from jax import lax
from jax.experimental import pallas as pl
from jax.experimental.pallas import tpu as pltpu
from jax.sharding import PartitionSpec as P

MESH = pl.DeviceIdType.MESH
f32, bf16 = jnp.float32, jnp.bfloat16
NEG = -1e30
NY, NX = 8, 4
BLOCK = 12
WINDOW = 64
R = 256
ROWS = 4096
TOKENS = R // 16
CHUNKS = ROWS // R
C = math.log2(math.e) / math.sqrt(128.0)


def dot_t(a, b):
    return lax.dot_general(a, b, (((1,), (1,)), ((), ())), preferred_element_type=f32)


def dot(a, b):
    return lax.dot_general(a, b, (((1,), (0,)), ((), ())), preferred_element_type=f32)


def dot_0(a, b):
    return lax.dot_general(a, b, (((0,), (0,)), ((), ())), preferred_element_type=f32)


def pick(x):
    x = x.reshape(TOKENS, 2, 8, 256)
    return jnp.concatenate([x[:, 0:1, :, :128], x[:, 1:2, :, 128:]], axis=1).reshape(R, 128)


def kernel(
    q_hbm, g_hbm, rk_ref, rv_ref, pk_ref, pv_ref, sk_ref, sv_ref, mask_ref, len_ref, cnt_ref,
    out_hbm, gk_ref, gv_ref,
    tmp, kx, vx, dv, q_ref, g_ref, o_ref, qe, ge, m1, l1, a1, e0, d0, wk, wv,
    gat, part, r1, r2, fin, acc_k, acc_v,
    in_sem, out_sem, z_send, z_recv, y_send, y_recv, x_send, x_recv, s_send, s_recv,
    r1_send, r1_recv, r2_send, r2_recv, r3_send, r3_recv,
):
    ctx, resp = lax.axis_index("ctx"), lax.axis_index("resp")
    y, core = ctx // 2, ctx % 2
    x, z = resp // 2, resp % 2

    q_copy = pltpu.make_async_copy(q_hbm, q_ref, in_sem.at[0])
    g_copy = pltpu.make_async_copy(g_hbm, g_ref, in_sem.at[1])
    q_copy.start()
    g_copy.start()

    barrier = pltpu.get_barrier_semaphore()

    def greet_ctx(k, c):
        pl.semaphore_signal(barrier, inc=1, device_id={"ctx": (ctx + k) % 16}, device_id_type=MESH)
        return c

    def greet_resp(k, c):
        pl.semaphore_signal(barrier, inc=1, device_id={"resp": (resp + k) % 8}, device_id_type=MESH)
        return c

    lax.fori_loop(1, 16, greet_ctx, 0)
    lax.fori_loop(1, 8, greet_resp, 0)

    def load2(ref, n):
        tmp[pl.ds(0, 2 * n), :] = ref[...].astype(f32)
        return tmp[pl.ds(0, n, stride=2), :], tmp[pl.ds(1, n, stride=2), :]

    k0, k1 = load2(sk_ref, BLOCK)
    v0, v1 = load2(sv_ref, BLOCK)
    mine = jnp.concatenate(
        [k0[:8], k1[:8], v0[:8], v1[:8], k0[8:], k1[8:], v0[8:], v1[8:]], axis=0
    ).astype(bf16)
    gat[ctx * 8 + resp] = mine

    pl.semaphore_wait(barrier, 22)

    def z_copy():
        b = ctx * 8 + resp
        return pltpu.make_async_remote_copy(
            src_ref=gat.at[b], dst_ref=gat.at[b], send_sem=z_send.at[0], recv_sem=z_recv.at[0],
            device_id={"resp": x * 2 + 1 - z}, device_id_type=MESH,
        )

    def y_copy(k):
        pair = gat.at[pl.ds(ctx * 8 + x * 2, 2)]
        return pltpu.make_async_remote_copy(
            src_ref=pair, dst_ref=pair, send_sem=y_send.at[k], recv_sem=y_recv.at[k],
            device_id={"ctx": ((y + k) % NY) * 2 + core}, device_id_type=MESH,
        )

    def x_copy(k, j):
        pair = gat.at[pl.ds(((y + NY - k) % NY) * 16 + core * 8 + x * 2, 2)]
        return pltpu.make_async_remote_copy(
            src_ref=pair, dst_ref=pair, send_sem=x_send.at[k, j], recv_sem=x_recv.at[k, j],
            device_id={"resp": ((x + j) % NX) * 2 + z}, device_id_type=MESH,
        )

    def s_copy(k):
        line = gat.at[pl.ds(((y + NY - k) % NY) * 16 + core * 8, 8)]
        return pltpu.make_async_remote_copy(
            src_ref=line, dst_ref=line, send_sem=s_send.at[k], recv_sem=s_recv.at[k],
            device_id={"ctx": y * 2 + 1 - core}, device_id_type=MESH,
        )

    z_copy().start()

    def both(ref, n):
        return jnp.concatenate(load2(ref, n), axis=1).astype(bf16)

    pk2, pv2 = both(pk_ref, 64), both(pv_ref, 64)
    z2 = jnp.zeros_like(pk2)
    kx[pl.ds(0, 64), :] = pk2
    kx[pl.ds(64, 64), :] = pk2
    vx[pl.ds(0, 64), :] = pv2
    vx[pl.ds(64, 64), :] = z2
    dv[pl.ds(0, 64), :] = z2
    dv[pl.ds(64, 64), :] = pv2
    kx[pl.ds(128, 256), :] = both(rk_ref, 256)
    vx[pl.ds(128, 256), :] = both(rv_ref, 256)
    length, count = len_ref[0], cnt_ref[0]
    lane = lax.broadcasted_iota(jnp.int32, (R, 128), 1)
    row = lax.broadcasted_iota(jnp.int32, (R, 1), 0)
    tok = lax.shift_right_logical(row, 4)
    head_hi = jnp.where((row & 8) == 8, 1.0, 0.0).astype(f32)
    hi = jnp.broadcast_to(head_hi, (R, 128)).astype(bf16)
    lo = jnp.broadcast_to(1.0 - head_hi, (R, 128)).astype(bf16)

    def own(i, nk):
        rows = pl.ds(pl.multiple_of(i * R, R), R)
        q = q_ref[rows, :]
        q2 = jnp.concatenate([q * lo, q * hi], axis=1)
        qe[rows, :] = q2
        t = tok + i * TOKENS
        live = jnp.where(t < length, 1.0, 0.0)
        g = (g_ref[rows, :].astype(f32) * live).astype(bf16)
        g2 = jnp.concatenate([g * lo, g * hi], axis=1)
        ge[rows, :] = g2
        s = dot_t(q2, kx[pl.ds(0, 128 + nk), :])
        last = jnp.minimum(t, length - 1)
        parts = [jnp.where((lane & 63) < count, s[:, :128], NEG)]
        for j in range(nk // 128):
            parts.append(jnp.where(lane + j * 128 <= last, s[:, 128 + j * 128 : 256 + j * 128], NEG))
        s = jnp.concatenate(parts, axis=1)
        m = jnp.max(s, axis=1, keepdims=True)
        p = jnp.exp2((s - m) * C)
        first = p[:, :128]
        tot = jnp.where(lane < 64, first, 0.0)
        for j in range(nk // 128):
            tot = tot + p[:, 128 + j * 128 : 256 + j * 128]
        l1[rows, :] = tot
        m1[rows, :] = m
        e0[rows, :] = first
        a1[rows, :] = pick(dot(p.astype(bf16), vx[pl.ds(0, 128 + nk), :]))
        d = dot_t(g2, dv[...])
        d0[rows, :] = jnp.where(lane < 64, 1.0, d)

    def run_own(lo_i, hi_i, nk):
        lax.fori_loop(lo_i, hi_i, lambda i, c: (own(i, nk), c)[1], 0)

    q_copy.wait()
    g_copy.wait()
    run_own(0, 1, 128)
    z_copy().wait()

    def start_y(k, c):
        y_copy(k).start()
        return c

    lax.fori_loop(1, NY, start_y, 0)
    for j in range(1, NX):
        x_copy(0, j).start()
    run_own(1, 4, 128)

    def pass_x(k, c):
        y_copy(k).wait_recv()
        for j in range(1, NX):
            x_copy(k, j).start()
        return c

    lax.fori_loop(1, NY, pass_x, 0)
    run_own(4, 8, 128)
    run_own(8, 12, 256)

    def pass_s(k, c):
        for j in range(1, NX):
            x_copy(k, j).wait_recv()
        s_copy(k).start()
        return c

    lax.fori_loop(0, NY, pass_s, 0)
    run_own(12, 16, 256)

    def end_gather(k, c):
        s_copy(k).wait()
        for j in range(1, NX):
            x_copy(k, j).wait_send()
        return c

    lax.fori_loop(0, NY, end_gather, 0)

    def end_y(k, c):
        y_copy(k).wait_send()
        return c

    lax.fori_loop(1, NY, end_y, 0)

    block_ids = lax.broadcasted_iota(jnp.int32, (1, 128), 1)
    first_block = jnp.min(jnp.where(mask_ref[...] == 1, block_ids, WINDOW))
    win = gat[pl.ds(first_block, WINDOW)].astype(f32)
    wk[pl.ds(0, 512), :] = jnp.concatenate([win[:, 0:8], win[:, 8:16]], axis=2).reshape(512, 256).astype(bf16)
    wv[pl.ds(0, 512), :] = jnp.concatenate([win[:, 16:24], win[:, 24:32]], axis=2).reshape(512, 256).astype(bf16)

    low4 = lax.broadcasted_iota(jnp.int32, (32, 8, 128), 1) < 4

    def rest(part4):
        part4 = part4.reshape(32, 2, 8, 128)
        b0, b1 = part4[:, 0], part4[:, 1]
        left = jnp.where(low4, b0, pltpu.roll(b1, 4, 1))
        right = jnp.where(low4, pltpu.roll(b0, 4, 1), b1)
        return jnp.concatenate([left, right], axis=2).reshape(256, 256).astype(bf16)

    wk[pl.ds(512, 256), :] = rest(win[:, 32:40])
    wv[pl.ds(512, 256), :] = rest(win[:, 40:48])

    acc_k[...] = jnp.zeros_like(acc_k)
    acc_v[...] = jnp.zeros_like(acc_v)

    def out_copy(i):
        rows = pl.ds(pl.multiple_of(i * R, R), R)
        return pltpu.make_async_copy(o_ref.at[rows], out_hbm.at[rows], out_sem.at[i])

    def prompt(i, c):
        rows = pl.ds(pl.multiple_of(i * R, R), R)
        q2, g2 = qe[rows, :], ge[rows, :]
        s = dot_t(q2, wk[...])
        mo = m1[rows, :]
        m = jnp.maximum(mo, jnp.max(s, axis=1, keepdims=True))
        p = jnp.exp2((s - m) * C)
        alpha = jnp.exp2((mo - m) * C)
        tot = l1[rows, :] * alpha
        for j in range(6):
            tot = tot + p[:, j * 128 : (j + 1) * 128]
        inv = 1.0 / jnp.sum(tot, axis=1, keepdims=True)
        mixed = (a1[rows, :] * alpha + pick(dot(p.astype(bf16), wv[...]))) * inv
        o_ref[rows, :] = mixed.astype(bf16)
        out_copy(i).start()
        g = (g2[:, :128] + g2[:, 128:]).astype(f32)
        inner = jnp.sum(g * mixed, axis=1, keepdims=True)
        ed = e0[rows, :] * (alpha * inv) * (d0[rows, :] - jnp.where(lane < 64, 0.0, inner))
        ed = ed.astype(bf16)
        acc_v[...] += dot_0(ed, g2)[:64]
        acc_k[...] += dot_0(ed, q2)[64:]
        return c

    lax.fori_loop(0, CHUNKS, prompt, 0)

    part[pl.ds(0, 4)] = acc_k[:, :128].astype(bf16).reshape(4, 16, 128)
    part[pl.ds(4, 4)] = acc_k[:, 128:].astype(bf16).reshape(4, 16, 128)
    part[pl.ds(8, 4)] = acc_v[:, :128].astype(bf16).reshape(4, 16, 128)
    part[pl.ds(12, 4)] = acc_v[:, 128:].astype(bf16).reshape(4, 16, 128)

    def r1_copy(k):
        to = (ctx + k) % 16
        return pltpu.make_async_remote_copy(
            src_ref=part.at[to], dst_ref=r1.at[k], send_sem=r1_send.at[k], recv_sem=r1_recv.at[k],
            device_id={"ctx": to}, device_id_type=MESH,
        )

    def r2_copy(k):
        return pltpu.make_async_remote_copy(
            src_ref=r2.at[resp], dst_ref=r2.at[resp], send_sem=r2_send.at[k], recv_sem=r2_recv.at[k],
            device_id={"resp": (resp + k) % 8}, device_id_type=MESH,
        )

    def r3_copy(k):
        return pltpu.make_async_remote_copy(
            src_ref=fin.at[ctx], dst_ref=fin.at[ctx], send_sem=r3_send.at[k], recv_sem=r3_recv.at[k],
            device_id={"ctx": (ctx + k) % 16}, device_id_type=MESH,
        )

    def each(copy, n, what):
        def step(k, c):
            getattr(copy(k), what)()
            return c

        lax.fori_loop(1, n, step, 0)

    each(r1_copy, 16, "start")
    total = part[ctx].astype(f32)
    each(r1_copy, 16, "wait_recv")
    for k in range(1, 16):
        total = total + r1[k].astype(f32)
    r2[resp] = total
    each(r2_copy, 8, "start")
    each(r2_copy, 8, "wait_recv")
    total = r2[0]
    for k in range(1, 8):
        total = total + r2[k]
    fin[ctx] = total
    each(r3_copy, 16, "start")
    each(r3_copy, 16, "wait_recv")
    for head in range(2):
        dst = pl.ds(head, 64, stride=2)
        gk_ref[dst, :] = fin[pl.ds(4 * head, 4)].reshape(64, 128) * (128.0 ** (-0.5))
        gv_ref[dst, :] = fin[pl.ds(8 + 4 * head, 4)].reshape(64, 128)
    each(r1_copy, 16, "wait_send")
    each(r2_copy, 8, "wait_send")
    each(r3_copy, 16, "wait_send")

    def end_out(i, c):
        out_copy(i).wait()
        return c

    lax.fori_loop(0, CHUNKS, end_out, 0)


def per_device(
    queries, prompt_k, prompt_v, resp_k, resp_v, prefix_k, prefix_v, d_out, shard_mask, resp_lengths, prefix_count
):
    vm = pl.BlockSpec(memory_space=pltpu.VMEM)
    sm = pl.BlockSpec(memory_space=pltpu.SMEM)
    hbm = pl.BlockSpec(memory_space=pl.ANY)
    vmem, dma = pltpu.VMEM, pltpu.SemaphoreType.DMA
    out, gk, gv = pl.pallas_call(
        kernel,
        out_shape=[
            jax.ShapeDtypeStruct((ROWS, 128), bf16),
            jax.ShapeDtypeStruct((128, 128), f32),
            jax.ShapeDtypeStruct((128, 128), f32),
        ],
        in_specs=[hbm, hbm] + [vm] * 7 + [sm, sm],
        out_specs=[hbm, vm, vm],
        scratch_shapes=[
            vmem((512, 128), f32), vmem((384, 256), bf16), vmem((384, 256), bf16), vmem((128, 256), bf16),
            vmem((ROWS, 128), bf16), vmem((ROWS, 128), bf16), vmem((ROWS, 128), bf16),
            vmem((ROWS, 256), bf16), vmem((ROWS, 256), bf16),
            vmem((ROWS, 1), f32), vmem((ROWS, 128), f32), vmem((ROWS, 128), f32),
            vmem((ROWS, 128), f32), vmem((ROWS, 128), f32),
            vmem((768, 256), bf16), vmem((768, 256), bf16),
            vmem((128, 48, 128), bf16),
            vmem((16, 16, 128), bf16), vmem((16, 16, 128), bf16), vmem((8, 16, 128), f32), vmem((16, 16, 128), f32),
            vmem((64, 256), f32), vmem((64, 256), f32),
            dma((2,)), dma((CHUNKS,)), dma((1,)), dma((1,)), dma((8,)), dma((8,)), dma((8, 4)), dma((8, 4)),
            dma((8,)), dma((8,)), dma((16,)), dma((16,)), dma((8,)), dma((8,)), dma((16,)), dma((16,)),
        ],
        compiler_params=pltpu.CompilerParams(
            collective_id=0, has_side_effects=True, vmem_limit_bytes=48 << 20
        ),
    )(
        queries.reshape(ROWS, 128), d_out.reshape(ROWS, 128), resp_k.reshape(512, 128), resp_v.reshape(512, 128),
        prefix_k.reshape(128, 128), prefix_v.reshape(128, 128), prompt_k.reshape(2 * BLOCK, 128),
        prompt_v.reshape(2 * BLOCK, 128), shard_mask, resp_lengths, prefix_count,
    )
    return out.reshape(256, 16, 128), gk.reshape(64, 2, 128), gv.reshape(64, 2, 128)


def solution(mesh):
    tokens = P(("ctx", "resp"), "head", None)
    prefix = P(None, "head", None)
    in_specs = (
        tokens, tokens, tokens, tokens, tokens, prefix, prefix, tokens,
        P(("ctx", "resp"), None), P(("ctx", "resp")), P(),
    )
    return jax.shard_map(
        per_device, mesh=mesh, in_specs=in_specs, out_specs=(tokens, prefix, prefix), check_vma=False
    )
```

time: 1580 us -> 75.2 us (0.05)
  waiting for transfers between devices: 952 us -> 0 us
  blocking collectives: 550 us -> 0 us
  Pallas kernels: 0 us -> 64.2 us
  matrix products: 40.6 us -> 0 us
    psum x1 -> x0, waiting for transfers between devices: 952 us -> none  [per_device(): grad_k, grad_v = lax.psum((grad_k, grad_v), ('ctx', 'resp'))]
    all_gather x2 -> x0, blocking collectives: 550 us -> none  [the longest x1 277 us: per_device(): lax.all_gather(prompt_v, ('ctx', 'resp'), axis=0, tiled=True)]
    pallas_call x0 -> x1, Pallas kernels: none -> 64.2 us  [per_device(): pl.pallas_call(kernel, out_shape=[jax.ShapeDtypeStruct((ROWS, 128), bf16)...]
    dot_general x16 -> x0, matrix products: 40.6 us -> none  [the longest x4 26.3 us: add_values(): jnp.einsum('rgqk,kgd->rgqd', weights, value_block, preferred_element_type...]
  transfers between devices with their start and end apart: 1 -> 0, of which waited for: 1 -> 0; matrix products, arithmetic and copies ran while one was open for 0% -> 0% of each run, Pallas kernels for 0% -> 0%
where the time goes in v1:
time: 75.2 us; the launch traced here: 74.8 us
  Pallas kernels  64.2 us (85%)
  local copies, waits for them, and re-layouts  8.69 us (12%)
  between operations  1.97 us (3%)
    pallas_call x1, Pallas kernels, per_device(): pl.pallas_call(kernel, out_shape=[jax.ShapeDtypeStruct((ROWS, 128), bf16)...  64.2 us
    unnamed x21, local copies, waits for them, and re-layouts  8.69 us

profile of v1, /device:TPU:1, one launch (start us, length us, event | category | flops | bytes accessed | tf_op | source)
XLA Modules:
  0.0 74.8 jit_solution(14018767868601797375)
XLA Ops:
  1.9 0.0 copy-start.7
  1.9 0.0 copy-start.6
  1.9 0.0 copy-start.8
  2.0 0.7 copy-done.7
  2.6 0.0 copy-done.6
  2.6 0.0 copy-done.8
  2.6 0.0 copy-start
  2.6 1.2 %copy-done = bf16[256,16,128]{2,1,0:T(8,128)(2,1)S(1)} copy-done((bf16[256,16,128]{2,1,0:T(8,128)(2,1)S(1)}, bf16[256,16,128]{2,1,0:T(8,128)(2,1)}, u32[]{:S(2)}) %copy-start) | copy-done | bytes 1048600
  3.9 0.0 copy-start.1
  3.9 1.2 %copy-done.1 = bf16[256,16,128]{2,1,0:T(8,128)(2,1)S(1)} copy-done((bf16[256,16,128]{2,1,0:T(8,128)(2,1)S(1)}, bf16[256,16,128]{2,1,0:T(8,128)(2,1)}, u32[]{:S(2)}) %copy-start.1) | copy-done | bytes 1048600
  5.1 0.0 copy-start.2
  5.1 0.9 %copy-done.2 = bf16[256,2,128]{2,1,0:T(2,128)(2,1)S(1)} copy-done((bf16[256,2,128]{2,1,0:T(2,128)(2,1)S(1)}, bf16[256,2,128]{2,1,0:T(2,128)(2,1)}, u32[]{:S(2)}) %copy-start.2) | copy-done | bytes 131096
  6.0 0.0 copy-start.3
  6.0 0.9 %copy-done.3 = bf16[256,2,128]{2,1,0:T(2,128)(2,1)S(1)} copy-done((bf16[256,2,128]{2,1,0:T(2,128)(2,1)S(1)}, bf16[256,2,128]{2,1,0:T(2,128)(2,1)}, u32[]{:S(2)}) %copy-start.3) | copy-done | bytes 131096
  6.9 0.0 copy-start.4
  6.9 0.8 %copy-done.4 = bf16[64,2,128]{2,1,0:T(2,128)(2,1)S(1)} copy-done((bf16[64,2,128]{2,1,0:T(2,128)(2,1)S(1)}, bf16[64,2,128]{2,1,0:T(2,128)(2,1)}, u32[]{:S(2)}) %copy-start.4) | copy-done | bytes 32792
  7.7 0.0 copy-start.5
  7.7 0.8 %copy-done.5 = bf16[64,2,128]{2,1,0:T(2,128)(2,1)S(1)} copy-done((bf16[64,2,128]{2,1,0:T(2,128)(2,1)S(1)}, bf16[64,2,128]{2,1,0:T(2,128)(2,1)}, u32[]{:S(2)}) %copy-start.5) | copy-done | bytes 32792
  8.4 64.2 %shard_map.130 = (bf16[4096,128]{1,0:T(8,128)(2,1)S(1)}, f32[128,128]{1,0:T(8,128)S(1)}, f32[128,128]{1,0:T(8,128)S(1)}) custom-call(bf16[4096,128]{1,0:T(8,128)(2,1)S(1)} %bitcast.11, bf16[4096,128]{1,0:T(8,128)(2,1)S(1)} %bitcast.12, bf16[512,128]{1,0:T(8,128)(2,1)S(1)} %bitcast.14, bf16[512,128]{1,0:T(8,128)(2,1)S(1)} %bitcast.15, ...), custom_call_target="tpu_custom_call" | custom-call | tf_op jit(solution)/shard_map/pallas_call | solution.py:331
  72.6 1.0 %copy.19 = bf16[256,16,128]{2,1,0:T(8,128)(2,1)} copy(bf16[256,16,128]{2,1,0:T(8,128)(2,1)S(1)} %bitcast.13) | data formatting | bytes 2097152
  73.6 0.6 copy.20
  74.2 0.6 copy.21
Async XLA Ops:
  1.9 0.7 copy-start.7
  1.9 0.7 copy-start.6
  1.9 0.7 copy-start.8
  2.6 1.2 %copy-start = (bf16[256,16,128]{2,1,0:T(8,128)(2,1)S(1)}, bf16[256,16,128]{2,1,0:T(8,128)(2,1)}, u32[]{:S(2)}) copy-start(bf16[256,16,128]{2,1,0:T(8,128)(2,1)} %param.11) | copy-start | bytes 3145732
  3.9 1.2 %copy-start.1 = (bf16[256,16,128]{2,1,0:T(8,128)(2,1)S(1)}, bf16[256,16,128]{2,1,0:T(8,128)(2,1)}, u32[]{:S(2)}) copy-start(bf16[256,16,128]{2,1,0:T(8,128)(2,1)} %param.18) | copy-start | bytes 3145732
  5.1 0.9 %copy-start.2 = (bf16[256,2,128]{2,1,0:T(2,128)(2,1)S(1)}, bf16[256,2,128]{2,1,0:T(2,128)(2,1)}, u32[]{:S(2)}) copy-start(bf16[256,2,128]{2,1,0:T(2,128)(2,1)} %param.14) | copy-start | bytes 393220
  6.0 0.9 %copy-start.3 = (bf16[256,2,128]{2,1,0:T(2,128)(2,1)S(1)}, bf16[256,2,128]{2,1,0:T(2,128)(2,1)}, u32[]{:S(2)}) copy-start(bf16[256,2,128]{2,1,0:T(2,128)(2,1)} %param.15) | copy-start | bytes 393220
  6.9 0.8 %copy-start.4 = (bf16[64,2,128]{2,1,0:T(2,128)(2,1)S(1)}, bf16[64,2,128]{2,1,0:T(2,128)(2,1)}, u32[]{:S(2)}) copy-start(bf16[64,2,128]{2,1,0:T(2,128)(2,1)} %param.16) | copy-start | bytes 98308
  7.7 0.8 %copy-start.5 = (bf16[64,2,128]{2,1,0:T(2,128)(2,1)S(1)}, bf16[64,2,128]{2,1,0:T(2,128)(2,1)}, u32[]{:S(2)}) copy-start(bf16[64,2,128]{2,1,0:T(2,128)(2,1)} %param.17) | copy-start | bytes 98308

commit v2 on v1

v2 whole, which is shorter than its diff:
```python
import functools
import math

import jax
import jax.numpy as jnp
from jax import lax
from jax.experimental import pallas as pl
from jax.experimental.pallas import tpu as pltpu
from jax.sharding import PartitionSpec as P

MESH = pl.DeviceIdType.MESH
f32, bf16 = jnp.float32, jnp.bfloat16
NEG = -1e30
NY, NX = 8, 4
BLOCK = 12
WINDOW = 64
R = 512
ROWS = 4096
TOKENS = R // 16
CHUNKS = ROWS // R
C = math.log2(math.e) / math.sqrt(128.0)


def dot_t(a, b):
    return lax.dot_general(a, b, (((1,), (1,)), ((), ())), preferred_element_type=f32)


def dot(a, b):
    return lax.dot_general(a, b, (((1,), (0,)), ((), ())), preferred_element_type=f32)


def dot_0(a, b):
    return lax.dot_general(a, b, (((0,), (0,)), ((), ())), preferred_element_type=f32)


def pick(x):
    x = x.reshape(TOKENS, 2, 8, 256)
    return jnp.concatenate([x[:, 0:1, :, :128], x[:, 1:2, :, 128:]], axis=1).reshape(R, 128)


def kernel(
    q_hbm, g_hbm, rk_hbm, rv_hbm, pk_hbm, pv_hbm, sk_hbm, sv_hbm, mask_hbm, len_hbm, cnt_hbm,
    o_ref, gk_ref, gv_ref,
    tmp, kx, vx, dv, q_ref, g_ref, rk_ref, rv_ref, pk_ref, pv_ref, sk_ref, sv_ref,
    mask_ref, len_ref, cnt_ref, qe, ge, m1, l1, a1, e0, d0, wk, wv,
    s1, s2, m2, gat, part, r1, r2, fin, acc_k, acc_v,
    in_sem, y_send, y_recv, x_send, x_recv, s_send, s_recv,
    r1_send, r1_recv, r2_send, r2_recv, r3_send, r3_recv,
):
    ctx, resp = lax.axis_index("ctx"), lax.axis_index("resp")
    y, core = ctx // 2, ctx % 2
    x, z = resp // 2, resp % 2

    loads = [
        pltpu.make_async_copy(src, dst, in_sem.at[n])
        for n, (src, dst) in enumerate(
            [
                (sk_hbm, sk_ref), (sv_hbm, sv_ref), (pk_hbm, pk_ref), (pv_hbm, pv_ref), (rk_hbm, rk_ref),
                (rv_hbm, rv_ref), (len_hbm, len_ref), (cnt_hbm, cnt_ref), (mask_hbm, mask_ref),
                (q_hbm, q_ref), (g_hbm, g_ref),
            ]
        )
    ]
    for load in loads:
        load.start()

    barrier = pltpu.get_barrier_semaphore()

    def peer_xzc(k):
        i = (resp * 2 + core + k) % 16
        return {"ctx": y * 2 + i % 2, "resp": i // 2}

    def peer_yz(k, j):
        return {"ctx": ((y + k) % NY) * 2 + core, "resp": x * 2 + (z + j) % 2}

    def greet_xzc(k, c):
        pl.semaphore_signal(barrier, inc=1, device_id=peer_xzc(k), device_id_type=MESH)
        return c

    def greet_yz(k, c):
        for j in range(2):
            pl.semaphore_signal(barrier, inc=1, device_id=peer_yz(k, j), device_id_type=MESH)
        return c

    lax.fori_loop(1, NY, greet_yz, 0)
    lax.fori_loop(1, 16, greet_xzc, 0)

    def load2(ref, n):
        tmp[pl.ds(0, 2 * n), :] = ref[...].astype(f32)
        return tmp[pl.ds(0, n, stride=2), :], tmp[pl.ds(1, n, stride=2), :]

    for load in loads[:2]:
        load.wait()
    k0, k1 = load2(sk_ref, BLOCK)
    v0, v1 = load2(sv_ref, BLOCK)
    mine = jnp.concatenate(
        [k0[:8], k1[:8], v0[:8], v1[:8], k0[8:], k1[8:], v0[8:], v1[8:]], axis=0
    ).astype(bf16)
    gat[ctx * 8 + resp] = mine

    def both(ref, n):
        return jnp.concatenate(load2(ref, n), axis=1).astype(bf16)

    for load in loads[2:9]:
        load.wait()
    pk2, pv2 = both(pk_ref, 64), both(pv_ref, 64)
    z2 = jnp.zeros_like(pk2)
    kx[pl.ds(0, 64), :] = pk2
    kx[pl.ds(64, 64), :] = pk2
    vx[pl.ds(0, 64), :] = pv2
    vx[pl.ds(64, 64), :] = z2
    dv[pl.ds(0, 64), :] = z2
    dv[pl.ds(64, 64), :] = pv2
    kx[pl.ds(128, 256), :] = both(rk_ref, 256)
    vx[pl.ds(128, 256), :] = both(rv_ref, 256)
    length, count = len_ref[0], cnt_ref[0]
    lane = lax.broadcasted_iota(jnp.int32, (R, 128), 1)
    row = lax.broadcasted_iota(jnp.int32, (R, 1), 0)
    tok = lax.shift_right_logical(row, 4)
    head_hi = jnp.where((row & 8) == 8, 1.0, 0.0).astype(f32)
    hi = jnp.broadcast_to(head_hi, (R, 128)).astype(bf16)
    lo = jnp.broadcast_to(1.0 - head_hi, (R, 128)).astype(bf16)

    def own_scores(i, nk, slot):
        rows = pl.ds(pl.multiple_of(i * R, R), R)
        q = q_ref[rows, :]
        q2 = jnp.concatenate([q * lo, q * hi], axis=1)
        qe[rows, :] = q2
        last = jnp.minimum(tok + i * TOKENS, length - 1)
        s = dot_t(q2, kx[pl.ds(0, 128 + nk), :])
        parts = [jnp.where((lane & 63) < count, s[:, :128], NEG)]
        for j in range(nk // 128):
            parts.append(jnp.where(lane + j * 128 <= last, s[:, 128 + j * 128 : 256 + j * 128], NEG))
        top = parts[0]
        for piece in parts[1:]:
            top = jnp.maximum(top, piece)
        m1[rows, :] = jnp.max(top, axis=1, keepdims=True)
        for j, piece in enumerate(parts):
            s1[slot, :, pl.ds(j * 128, 128)] = piece

    def own_values(i, nk, slot):
        rows = pl.ds(pl.multiple_of(i * R, R), R)
        live = jnp.where(tok + i * TOKENS < length, 1.0, 0.0)
        g = (g_ref[rows, :].astype(f32) * live).astype(bf16)
        g2 = jnp.concatenate([g * lo, g * hi], axis=1)
        ge[rows, :] = g2
        p = jnp.exp2((s1[slot, :, pl.ds(0, 128 + nk)] - m1[rows, :]) * C)
        first = p[:, :128]
        tot = jnp.where(lane < 64, first, 0.0)
        for j in range(nk // 128):
            tot = tot + p[:, 128 + j * 128 : 256 + j * 128]
        l1[rows, :] = tot
        e0[rows, :] = first
        a1[rows, :] = pick(dot(p.astype(bf16), vx[pl.ds(0, 128 + nk), :]))
        d0[rows, :] = jnp.where(lane < 64, 1.0, dot_t(g2, dv[...]))

    def staggered(scores, values, first, last):
        scores(first, 0)

        def two(j, c):
            i = first + 2 * j
            scores(i + 1, 1)
            values(i, 0)
            scores(i + 2, 0)
            values(i + 1, 1)
            return c

        lax.fori_loop(0, (last - first) // 2 - 1, two, 0)
        scores(last - 1, 1)
        values(last - 2, 0)
        values(last - 1, 1)

    def run_own(first, last, nk):
        staggered(lambda i, slot: own_scores(i, nk, slot), lambda i, slot: own_values(i, nk, slot), first, last)

    for load in loads[9:]:
        load.wait()
    run_own(0, CHUNKS // 2, 128)

    pl.semaphore_wait(barrier, 29)

    def y_copy(k, j):
        b = ctx * 8 + resp
        return pltpu.make_async_remote_copy(
            src_ref=gat.at[b], dst_ref=gat.at[b], send_sem=y_send.at[k, j], recv_sem=y_recv.at[k, j],
            device_id=peer_yz(k, j), device_id_type=MESH,
        )

    def x_copy(k, j):
        pair = gat.at[pl.ds(((y + NY - k) % NY) * 16 + core * 8 + x * 2, 2)]
        return pltpu.make_async_remote_copy(
            src_ref=pair, dst_ref=pair, send_sem=x_send.at[k, j], recv_sem=x_recv.at[k, j],
            device_id={"resp": ((x + j) % NX) * 2 + z}, device_id_type=MESH,
        )

    def s_copy(k):
        line = gat.at[pl.ds(((y + NY - k) % NY) * 16 + core * 8, 8)]
        return pltpu.make_async_remote_copy(
            src_ref=line, dst_ref=line, send_sem=s_send.at[k], recv_sem=s_recv.at[k],
            device_id={"ctx": y * 2 + 1 - core}, device_id_type=MESH,
        )

    def near_first(n):
        return lax.rem((n + 1) // 2 * (n % 2) + (NY - n // 2) * (1 - n % 2), NY)

    y_copy(0, 1).start()

    def start_y(n, c):
        k = near_first(n)
        y_copy(k, 0).start()
        y_copy(k, 1).start()
        return c

    lax.fori_loop(1, NY, start_y, 0)

    def pass_x(n, c):
        k = near_first(n)
        y_copy(k, 1).wait_recv()

        @pl.when(n > 0)
        def _():
            y_copy(k, 0).wait_recv()

        for j in (1, 3, 2):
            x_copy(k, j).start()
        return c

    def pass_s(n, c):
        k = near_first(n)
        for j in range(1, NX):
            x_copy(k, j).wait_recv()
        s_copy(k).start()
        return c

    run_own(CHUNKS // 2, CHUNKS, 256)
    lax.fori_loop(0, NY, pass_x, 0)
    lax.fori_loop(0, NY, pass_s, 0)

    def end_gather(k, c):
        s_copy(k).wait()
        for j in range(1, NX):
            x_copy(k, j).wait_send()
        y_copy(k, 1).wait_send()

        @pl.when(k > 0)
        def _():
            y_copy(k, 0).wait_send()

        return c

    lax.fori_loop(0, NY, end_gather, 0)

    block_ids = lax.broadcasted_iota(jnp.int32, (1, 128), 1)
    first_block = jnp.min(jnp.where(mask_ref[...] == 1, block_ids, WINDOW))
    win = gat[pl.ds(first_block, WINDOW)].astype(f32)
    wk[pl.ds(0, 512), :] = jnp.concatenate([win[:, 0:8], win[:, 8:16]], axis=2).reshape(512, 256).astype(bf16)
    wv[pl.ds(0, 512), :] = jnp.concatenate([win[:, 16:24], win[:, 24:32]], axis=2).reshape(512, 256).astype(bf16)

    low4 = lax.broadcasted_iota(jnp.int32, (32, 8, 128), 1) < 4

    def rest(part4):
        part4 = part4.reshape(32, 2, 8, 128)
        b0, b1 = part4[:, 0], part4[:, 1]
        left = jnp.where(low4, b0, pltpu.roll(b1, 4, 1))
        right = jnp.where(low4, pltpu.roll(b0, 4, 1), b1)
        return jnp.concatenate([left, right], axis=2).reshape(256, 256).astype(bf16)

    wk[pl.ds(512, 256), :] = rest(win[:, 32:40])
    wv[pl.ds(512, 256), :] = rest(win[:, 40:48])

    acc_k[...] = jnp.zeros_like(acc_k)
    acc_v[...] = jnp.zeros_like(acc_v)

    def prompt_scores(i, slot):
        rows = pl.ds(pl.multiple_of(i * R, R), R)
        s = dot_t(qe[rows, :], wk[...])
        s2[slot] = s
        top = s[:, :128]
        for j in range(1, 6):
            top = jnp.maximum(top, s[:, j * 128 : (j + 1) * 128])
        m2[slot] = jnp.maximum(m1[rows, :], jnp.max(top, axis=1, keepdims=True))

    def prompt_values(i, slot):
        rows = pl.ds(pl.multiple_of(i * R, R), R)
        q2, g2 = qe[rows, :], ge[rows, :]
        mo, m = m1[rows, :], m2[slot]
        p = jnp.exp2((s2[slot] - m) * C)
        alpha = jnp.exp2((mo - m) * C)
        tot = l1[rows, :] * alpha
        for j in range(6):
            tot = tot + p[:, j * 128 : (j + 1) * 128]
        inv = 1.0 / jnp.sum(tot, axis=1, keepdims=True)
        mixed = (a1[rows, :] * alpha + pick(dot(p.astype(bf16), wv[...]))) * inv
        o_ref[rows, :] = mixed.astype(bf16)
        g = (g2[:, :128] + g2[:, 128:]).astype(f32)
        inner = jnp.sum(g * mixed, axis=1, keepdims=True)
        ed = e0[rows, :] * (alpha * inv) * (d0[rows, :] - jnp.where(lane < 64, 0.0, inner))
        ed = ed.astype(bf16)
        acc_v[...] += dot_0(ed, g2)[:64]
        acc_k[...] += dot_0(ed, q2)[64:]

    staggered(prompt_scores, prompt_values, 0, CHUNKS)

    part[pl.ds(0, 4)] = acc_k[:, :128].astype(bf16).reshape(4, 16, 128)
    part[pl.ds(4, 4)] = acc_k[:, 128:].astype(bf16).reshape(4, 16, 128)
    part[pl.ds(8, 4)] = acc_v[:, :128].astype(bf16).reshape(4, 16, 128)
    part[pl.ds(12, 4)] = acc_v[:, 128:].astype(bf16).reshape(4, 16, 128)

    seat = resp * 2 + core

    def r1_copy(k):
        return pltpu.make_async_remote_copy(
            src_ref=part.at[(seat + k) % 16], dst_ref=r1.at[k], send_sem=r1_send.at[k], recv_sem=r1_recv.at[k],
            device_id=peer_xzc(k), device_id_type=MESH,
        )

    def r2_copy(k):
        return pltpu.make_async_remote_copy(
            src_ref=r2.at[y], dst_ref=r2.at[y], send_sem=r2_send.at[k], recv_sem=r2_recv.at[k],
            device_id=peer_yz(k, 0), device_id_type=MESH,
        )

    def r3_copy(k):
        return pltpu.make_async_remote_copy(
            src_ref=fin.at[seat], dst_ref=fin.at[seat], send_sem=r3_send.at[k], recv_sem=r3_recv.at[k],
            device_id=peer_xzc(k), device_id_type=MESH,
        )

    def each(copy, n, what):
        def step(k, c):
            getattr(copy(k), what)()
            return c

        lax.fori_loop(1, n, step, 0)

    each(r1_copy, 16, "start")
    total = part[seat].astype(f32)
    each(r1_copy, 16, "wait_recv")
    for k in range(1, 16):
        total = total + r1[k].astype(f32)
    r2[y] = total
    each(r2_copy, 8, "start")
    each(r2_copy, 8, "wait_recv")
    total = r2[0]
    for k in range(1, 8):
        total = total + r2[k]
    fin[seat] = total
    each(r3_copy, 16, "start")
    each(r3_copy, 16, "wait_recv")
    for head in range(2):
        dst = pl.ds(head, 64, stride=2)
        gk_ref[dst, :] = fin[pl.ds(4 * head, 4)].reshape(64, 128) * (128.0 ** (-0.5))
        gv_ref[dst, :] = fin[pl.ds(8 + 4 * head, 4)].reshape(64, 128)
    each(r1_copy, 16, "wait_send")
    each(r2_copy, 8, "wait_send")
    each(r3_copy, 16, "wait_send")


def place(o_ref, k_ref, v_ref, out_ref, gk_ref, gv_ref, sem):
    n = ROWS // 4
    copies = [pltpu.make_async_copy(k_ref, gk_ref, sem.at[4]), pltpu.make_async_copy(v_ref, gv_ref, sem.at[5])]
    for i in range(4):
        rows = pl.ds(i * n, n)
        copies.append(pltpu.make_async_copy(o_ref.at[rows], out_ref.at[rows], sem.at[i]))
    for copy in copies:
        copy.start()
    for copy in copies:
        copy.wait()


def per_device(
    queries, prompt_k, prompt_v, resp_k, resp_v, prefix_k, prefix_v, d_out, shard_mask, resp_lengths, prefix_count
):
    vm = pl.BlockSpec(memory_space=pltpu.VMEM)
    hbm = pl.BlockSpec(memory_space=pltpu.HBM)
    vmem, dma = pltpu.VMEM, pltpu.SemaphoreType.DMA
    out, gk, gv = pl.pallas_call(
        kernel,
        out_shape=[vmem((ROWS, 128), bf16), vmem((128, 128), f32), vmem((128, 128), f32)],
        in_specs=[hbm] * 11,
        out_specs=[vm] * 3,
        scratch_shapes=[
            vmem((512, 128), f32), vmem((384, 256), bf16), vmem((384, 256), bf16), vmem((128, 256), bf16),
            vmem((ROWS, 128), bf16), vmem((ROWS, 128), bf16), vmem((512, 128), bf16), vmem((512, 128), bf16),
            vmem((128, 128), bf16), vmem((128, 128), bf16), vmem((2 * BLOCK, 128), bf16), vmem((2 * BLOCK, 128), bf16),
            vmem((1, 128), jnp.int32), pltpu.SMEM((1,), jnp.int32), pltpu.SMEM((1,), jnp.int32),
            vmem((ROWS, 256), bf16), vmem((ROWS, 256), bf16),
            vmem((ROWS, 1), f32), vmem((ROWS, 128), f32), vmem((ROWS, 128), f32),
            vmem((ROWS, 128), f32), vmem((ROWS, 128), f32),
            vmem((768, 256), bf16), vmem((768, 256), bf16),
            vmem((2, R, 384), f32), vmem((2, R, 768), f32), vmem((2, R, 1), f32),
            vmem((128, 48, 128), bf16),
            vmem((16, 16, 128), bf16), vmem((16, 16, 128), bf16), vmem((8, 16, 128), f32), vmem((16, 16, 128), f32),
            vmem((64, 256), f32), vmem((64, 256), f32),
            dma((11,)), dma((8, 2)), dma((8, 2)), dma((8, 4)), dma((8, 4)),
            dma((8,)), dma((8,)), dma((16,)), dma((16,)), dma((8,)), dma((8,)), dma((16,)), dma((16,)),
        ],
        compiler_params=pltpu.CompilerParams(
            collective_id=0, has_side_effects=True, vmem_limit_bytes=60 << 20
        ),
    )(
        queries.reshape(ROWS, 128), d_out.reshape(ROWS, 128), resp_k.reshape(512, 128), resp_v.reshape(512, 128),
        prefix_k.reshape(128, 128), prefix_v.reshape(128, 128), prompt_k.reshape(2 * BLOCK, 128),
        prompt_v.reshape(2 * BLOCK, 128), shard_mask, resp_lengths, prefix_count,
    )
    out, gk, gv = pl.pallas_call(
        place,
        out_shape=[
            jax.ShapeDtypeStruct((ROWS, 128), bf16),
            jax.ShapeDtypeStruct((128, 128), f32),
            jax.ShapeDtypeStruct((128, 128), f32),
        ],
        in_specs=[vm] * 3,
        out_specs=[hbm] * 3,
        scratch_shapes=[dma((6,))],
        compiler_params=pltpu.CompilerParams(vmem_limit_bytes=16 << 20),
    )(out, gk, gv)
    return out.reshape(256, 16, 128), gk.reshape(64, 2, 128), gv.reshape(64, 2, 128)


def solution(mesh):
    tokens = P(("ctx", "resp"), "head", None)
    prefix = P(None, "head", None)
    in_specs = (
        tokens, tokens, tokens, tokens, tokens, prefix, prefix, tokens,
        P(("ctx", "resp"), None), P(("ctx", "resp")), P(),
    )
    return jax.shard_map(
        per_device, mesh=mesh, in_specs=in_specs, out_specs=(tokens, prefix, prefix), check_vma=False
    )
```

time: 75.2 us -> 52.7 us (0.70)
  Pallas kernels: 64.2 us -> 50.6 us
  local copies, waits for them, and re-layouts: 8.69 us -> 0 us
    pallas_call x1 -> x2, Pallas kernels: 64.2 us -> 50.6 us  [the longest x1 49.6 us: per_device(): pl.pallas_call(kernel, out_shape=[vmem((ROWS, 128), bf16), vmem((128, 128...]
    unnamed x21 -> x0, local copies, waits for them, and re-layouts: 8.69 us -> none
where the time goes in v2:
time: 52.7 us; the launch traced here: 52.5 us
  Pallas kernels  50.6 us (96%)
  between operations  1.93 us (4%)
    pallas_call x1, Pallas kernels, per_device(): pl.pallas_call(kernel, out_shape=[vmem((ROWS, 128), bf16), vmem((128, 128...  49.6 us
    pallas_call x1, Pallas kernels, per_device(): pl.pallas_call(place, out_shape=[jax.ShapeDtypeStruct((ROWS, 128), bf16),...  1.06 us

profile of v2, /device:TPU:1, one launch (start us, length us, event | category | flops | bytes accessed | tf_op | source)
XLA Modules:
  0.0 52.5 jit_solution(1185086220116155854)
XLA Ops:
  1.9 49.6 %shard_map.130 = (bf16[4096,128]{1,0:T(8,128)(2,1)S(1)}, f32[128,128]{1,0:T(8,128)S(1)}, f32[128,128]{1,0:T(8,128)S(1)}) custom-call(bf16[4096,128]{1,0:T(8,128)(2,1)} %bitcast.11, bf16[4096,128]{1,0:T(8,128)(2,1)} %bitcast.12, bf16[512,128]{1,0:T(8,128)(2,1)} %bitcast.13, bf16[512,128]{1,0:T(8,128)(2,1)} %bitcast.14, bf16[128,128]{1,0:T(8,128)(2,1)} %bitcast.15, ...), custom_call_target="tpu_custom_call" | custom-call | tf_op jit(solution)/shard_map/pallas_call | solution.py:377
  51.5 1.1 %shard_map.131 = (bf16[4096,128]{1,0:T(8,128)(2,1)}, f32[128,128]{1,0:T(8,128)}, f32[128,128]{1,0:T(8,128)}) custom-call(bf16[4096,128]{1,0:T(8,128)(2,1)S(1)} %get-tuple-element.9.o_ref, f32[128,128]{1,0:T(8,128)S(1)} %get-tuple-element.10.k_ref, f32[128,128]{1,0:T(8,128)S(1)} %get-tuple-element.11.v_ref), custom_call_target="tpu_custom_call" | custom-call | tf_op jit(solution)/shard_map/pallas_call | solution.py:406

commit v3 on v2

--- a/solution.py
+++ b/solution.py
@@ -14,7 +14,8 @@
 NY, NX = 8, 4
 BLOCK = 12
 WINDOW = 64
-R = 512
+R = 1024
+NEAR = 4
 ROWS = 4096
 TOKENS = R // 16
 CHUNKS = ROWS // R
@@ -44,7 +45,7 @@
     tmp, kx, vx, dv, q_ref, g_ref, rk_ref, rv_ref, pk_ref, pv_ref, sk_ref, sv_ref,
     mask_ref, len_ref, cnt_ref, qe, ge, m1, l1, a1, e0, d0, wk, wv,
     s1, s2, m2, gat, part, r1, r2, fin, acc_k, acc_v,
-    in_sem, y_send, y_recv, x_send, x_recv, s_send, s_recv,
+    in_sem, y_send, y_recv, x_send, x_recv, z_send, z_recv, s_send, s_recv,
     r1_send, r1_recv, r2_send, r2_recv, r3_send, r3_recv,
 ):
     ctx, resp = lax.axis_index("ctx"), lax.axis_index("resp")
@@ -82,8 +83,8 @@
             pl.semaphore_signal(barrier, inc=1, device_id=peer_yz(k, j), device_id_type=MESH)
         return c
 
-    lax.fori_loop(1, NY, greet_yz, 0)
-    lax.fori_loop(1, 16, greet_xzc, 0)
+    lax.fori_loop(1, NY, lambda i, c: greet_yz(lax.rem(i + 2, NY) + (i + 2) // NY, c), 0)
+    lax.fori_loop(1, 16, lambda i, c: greet_xzc(lax.rem(i + 7, 16) + (i + 7) // 16, c), 0)
 
     def load2(ref, n):
         tmp[pl.ds(0, 2 * n), :] = ref[...].astype(f32)
@@ -134,7 +135,7 @@
         top = parts[0]
         for piece in parts[1:]:
             top = jnp.maximum(top, piece)
-        m1[rows, :] = jnp.max(top, axis=1, keepdims=True)
+        m1[rows, :] = jnp.broadcast_to(jnp.max(top, axis=1, keepdims=True), (R, 128))
         for j, piece in enumerate(parts):
             s1[slot, :, pl.ds(j * 128, 128)] = piece
 
@@ -144,7 +145,9 @@
         g = (g_ref[rows, :].astype(f32) * live).astype(bf16)
         g2 = jnp.concatenate([g * lo, g * hi], axis=1)
         ge[rows, :] = g2
-        p = jnp.exp2((s1[slot, :, pl.ds(0, 128 + nk)] - m1[rows, :]) * C)
+        m = m1[rows, :]
+        cols = [jnp.exp2((s1[slot, :, pl.ds(j * 128, 128)] - m) * C) for j in range(1 + nk // 128)]
+        p = jnp.concatenate(cols, axis=1)
         first = p[:, :128]
         tot = jnp.where(lane < 64, first, 0.0)
         for j in range(nk // 128):
@@ -179,76 +182,104 @@
 
     pl.semaphore_wait(barrier, 29)
 
+    def remote(ref, sems, at, peer):
+        return pltpu.make_async_remote_copy(
+            src_ref=ref, dst_ref=ref, send_sem=sems[0].at[at], recv_sem=sems[1].at[at],
+            device_id=peer, device_id_type=MESH,
+        )
+
+    def line(k):
+        return ((y + NY - k) % NY) * 16 + core * 8
+
     def y_copy(k, j):
-        b = ctx * 8 + resp
-        return pltpu.make_async_remote_copy(
-            src_ref=gat.at[b], dst_ref=gat.at[b], send_sem=y_send.at[k, j], recv_sem=y_recv.at[k, j],
-            device_id=peer_yz(k, j), device_id_type=MESH,
-        )
-
-    def x_copy(k, j):
-        pair = gat.at[pl.ds(((y + NY - k) % NY) * 16 + core * 8 + x * 2, 2)]
-        return pltpu.make_async_remote_copy(
-            src_ref=pair, dst_ref=pair, send_sem=x_send.at[k, j], recv_sem=x_recv.at[k, j],
-            device_id={"resp": ((x + j) % NX) * 2 + z}, device_id_type=MESH,
-        )
+        return remote(gat.at[ctx * 8 + resp], (y_send, y_recv), (k, j), peer_yz(k, j))
+
+    def x_copy(k, j, n):
+        first = line(k) + x * 2
+        ref = gat.at[pl.ds(first, 2)] if n == 2 else gat.at[pl.ds(first + z, 1)]
+        return remote(ref, (x_send, x_recv), (k, j), {"resp": ((x + j) % NX) * 2 + z})
+
+    def z_copy(k, j):
+        ref = gat.at[line(k) + ((x + NX - j) % NX) * 2 + z]
+        return remote(ref, (z_send, z_recv), (k, j), {"resp": x * 2 + 1 - z})
 
     def s_copy(k):
-        line = gat.at[pl.ds(((y + NY - k) % NY) * 16 + core * 8, 8)]
-        return pltpu.make_async_remote_copy(
-            src_ref=line, dst_ref=line, send_sem=s_send.at[k], recv_sem=s_recv.at[k],
-            device_id={"ctx": y * 2 + 1 - core}, device_id_type=MESH,
-        )
-
-    def near_first(n):
+        return remote(gat.at[pl.ds(line(k), 8)], (s_send, s_recv), (k,), {"ctx": y * 2 + 1 - core})
+
+    def at_distance(n):
         return lax.rem((n + 1) // 2 * (n % 2) + (NY - n // 2) * (1 - n % 2), NY)
 
-    y_copy(0, 1).start()
-
-    def start_y(n, c):
-        k = near_first(n)
-        y_copy(k, 0).start()
-        y_copy(k, 1).start()
+    def loop(first, last, step):
+        def body(n, c):
+            step(at_distance(n))
+            return c
+
+        lax.fori_loop(first, last, body, 0)
+
+    def send_near(k):
+        for j in (2, 1, 3):
+            x_copy(k, j, 1).start()
+        z_copy(k, 0).start()
+
+    def pass_near(k):
+        y_copy(k, 0).wait_recv()
+        send_near(k)
+
+    def pass_far(k):
+        for j in range(2):
+            y_copy(k, j).wait_recv()
+        for j in (2, 1, 3):
+            x_copy(k, j, 2).start()
+
+    def pass_z(k):
+        for j in (1, 3, 2):
+            x_copy(k, j, 1).wait_recv()
+            z_copy(k, j).start()
+
+    def line_near(k):
+        for j in range(NX):
+            z_copy(k, j).wait_recv()
+        s_copy(k).start()
+
+    def line_far(k):
+        for j in (1, 3, 2):
+            x_copy(k, j, 2).wait_recv()
+        s_copy(k).start()
+
+    def start_far(n, c):
+        k = at_distance(NY - 1 - n)
+        for j in range(2):
+            y_copy(k, j).start()
         return c
 
-    lax.fori_loop(1, NY, start_y, 0)
-
-    def pass_x(n, c):
-        k = near_first(n)
-        y_copy(k, 1).wait_recv()
-
-        @pl.when(n > 0)
-        def _():
-            y_copy(k, 0).wait_recv()
-
-        for j in (1, 3, 2):
-            x_copy(k, j).start()
-        return c
-
-    def pass_s(n, c):
-        k = near_first(n)
+    lax.fori_loop(0, NY - NEAR, start_far, 0)
+    loop(1, NEAR, lambda k: y_copy(k, 0).start())
+    send_near(0)
+    run_own(CHUNKS // 2, CHUNKS, 256)
+    loop(1, NEAR, pass_near)
+    pass_z(0)
+    loop(NEAR, NY, pass_far)
+    loop(1, NEAR, pass_z)
+    loop(0, NEAR, line_near)
+    loop(NEAR, NY, line_far)
+
+    def end_near(k):
         for j in range(1, NX):
-            x_copy(k, j).wait_recv()
-        s_copy(k).start()
-        return c
-
-    run_own(CHUNKS // 2, CHUNKS, 256)
-    lax.fori_loop(0, NY, pass_x, 0)
-    lax.fori_loop(0, NY, pass_s, 0)
-
-    def end_gather(k, c):
+            x_copy(k, j, 1).wait_send()
+        for j in range(NX):
+            z_copy(k, j).wait_send()
         s_copy(k).wait()
+
+    def end_far(k):
+        for j in range(2):
+            y_copy(k, j).wait_send()
         for j in range(1, NX):
-            x_copy(k, j).wait_send()
-        y_copy(k, 1).wait_send()
-
-        @pl.when(k > 0)
-        def _():
-            y_copy(k, 0).wait_send()
-
-        return c
-
-    lax.fori_loop(0, NY, end_gather, 0)
+            x_copy(k, j, 2).wait_send()
+        s_copy(k).wait()
+
+    loop(1, NEAR, lambda k: y_copy(k, 0).wait_send())
+    loop(0, NEAR, end_near)
+    loop(NEAR, NY, end_far)
 
     block_ids = lax.broadcasted_iota(jnp.int32, (1, 128), 1)
     first_block = jnp.min(jnp.where(mask_ref[...] == 1, block_ids, WINDOW))
@@ -278,13 +309,14 @@
         top = s[:, :128]
         for j in range(1, 6):
             top = jnp.maximum(top, s[:, j * 128 : (j + 1) * 128])
-        m2[slot] = jnp.maximum(m1[rows, :], jnp.max(top, axis=1, keepdims=True))
+        m2[slot] = jnp.maximum(m1[rows, :], jnp.broadcast_to(jnp.max(top, axis=1, keepdims=True), (R, 128)))
 
     def prompt_values(i, slot):
         rows = pl.ds(pl.multiple_of(i * R, R), R)
         q2, g2 = qe[rows, :], ge[rows, :]
         mo, m = m1[rows, :], m2[slot]
-        p = jnp.exp2((s2[slot] - m) * C)
+        cols = [jnp.exp2((s2[slot, :, pl.ds(j * 128, 128)] - m) * C) for j in range(6)]
+        p = jnp.concatenate(cols, axis=1)
         alpha = jnp.exp2((mo - m) * C)
         tot = l1[rows, :] * alpha
         for j in range(6):
@@ -327,30 +359,30 @@
         )
 
     def each(copy, n, what):
-        def step(k, c):
-            getattr(copy(k), what)()
+        def step(i, c):
+            getattr(copy(lax.rem(i + n // 2, n) + i // (n // 2)), what)()
             return c
 
-        lax.fori_loop(1, n, step, 0)
+        lax.fori_loop(0, n - 1, step, 0)
 
     each(r1_copy, 16, "start")
     total = part[seat].astype(f32)
     each(r1_copy, 16, "wait_recv")
     for k in range(1, 16):
         total = total + r1[k].astype(f32)
-    r2[y] = total
+    r2[y] = total.astype(bf16)
     each(r2_copy, 8, "start")
     each(r2_copy, 8, "wait_recv")
-    total = r2[0]
+    total = r2[0].astype(f32)
     for k in range(1, 8):
-        total = total + r2[k]
-    fin[seat] = total
+        total = total + r2[k].astype(f32)
+    fin[seat] = total.astype(bf16)
     each(r3_copy, 16, "start")
     each(r3_copy, 16, "wait_recv")
     for head in range(2):
         dst = pl.ds(head, 64, stride=2)
-        gk_ref[dst, :] = fin[pl.ds(4 * head, 4)].reshape(64, 128) * (128.0 ** (-0.5))
-        gv_ref[dst, :] = fin[pl.ds(8 + 4 * head, 4)].reshape(64, 128)
+        gk_ref[dst, :] = fin[pl.ds(4 * head, 4)].astype(f32).reshape(64, 128) * (128.0 ** (-0.5))
+        gv_ref[dst, :] = fin[pl.ds(8 + 4 * head, 4)].astype(f32).reshape(64, 128)
     each(r1_copy, 16, "wait_send")
     each(r2_copy, 8, "wait_send")
     each(r3_copy, 16, "wait_send")
@@ -385,14 +417,14 @@
             vmem((128, 128), bf16), vmem((128, 128), bf16), vmem((2 * BLOCK, 128), bf16), vmem((2 * BLOCK, 128), bf16),
             vmem((1, 128), jnp.int32), pltpu.SMEM((1,), jnp.int32), pltpu.SMEM((1,), jnp.int32),
             vmem((ROWS, 256), bf16), vmem((ROWS, 256), bf16),
-            vmem((ROWS, 1), f32), vmem((ROWS, 128), f32), vmem((ROWS, 128), f32),
+            vmem((ROWS, 128), f32), vmem((ROWS, 128), f32), vmem((ROWS, 128), f32),
             vmem((ROWS, 128), f32), vmem((ROWS, 128), f32),
             vmem((768, 256), bf16), vmem((768, 256), bf16),
-            vmem((2, R, 384), f32), vmem((2, R, 768), f32), vmem((2, R, 1), f32),
+            vmem((2, R, 384), f32), vmem((2, R, 768), f32), vmem((2, R, 128), f32),
             vmem((128, 48, 128), bf16),
-            vmem((16, 16, 128), bf16), vmem((16, 16, 128), bf16), vmem((8, 16, 128), f32), vmem((16, 16, 128), f32),
+            vmem((16, 16, 128), bf16), vmem((16, 16, 128), bf16), vmem((8, 16, 128), bf16), vmem((16, 16, 128), bf16),
             vmem((64, 256), f32), vmem((64, 256), f32),
-            dma((11,)), dma((8, 2)), dma((8, 2)), dma((8, 4)), dma((8, 4)),
+            dma((11,)), dma((8, 2)), dma((8, 2)), dma((8, 4)), dma((8, 4)), dma((8, 4)), dma((8, 4)),
             dma((8,)), dma((8,)), dma((16,)), dma((16,)), dma((8,)), dma((8,)), dma((16,)), dma((16,)),
         ],
         compiler_params=pltpu.CompilerParams(

time: 52.7 us -> 49.8 us (0.945)
  Pallas kernels: 50.6 us -> 47.6 us
    pallas_call x1, Pallas kernels: 49.6 us -> 46.6 us  [per_device(): pl.pallas_call(kernel, out_shape=[vmem((ROWS, 128), bf16), vmem((128, 128...]
where the time goes in v3:
time: 49.8 us; the launch traced here: 49.6 us
  Pallas kernels  47.6 us (96%)
  between operations  1.93 us (4%)
    pallas_call x1, Pallas kernels, per_device(): pl.pallas_call(kernel, out_shape=[vmem((ROWS, 128), bf16), vmem((128, 128...  46.6 us
    pallas_call x1, Pallas kernels, per_device(): pl.pallas_call(place, out_shape=[jax.ShapeDtypeStruct((ROWS, 128), bf16),...  1.06 us

profile of v3, /device:TPU:1, one launch (start us, length us, event | category | flops | bytes accessed | tf_op | source)
XLA Modules:
  0.0 49.6 jit_solution(11321594573287851272)
XLA Ops:
  1.9 46.6 %shard_map.130 = (bf16[4096,128]{1,0:T(8,128)(2,1)S(1)}, f32[128,128]{1,0:T(8,128)S(1)}, f32[128,128]{1,0:T(8,128)S(1)}) custom-call(bf16[4096,128]{1,0:T(8,128)(2,1)} %bitcast.11, bf16[4096,128]{1,0:T(8,128)(2,1)} %bitcast.12, bf16[512,128]{1,0:T(8,128)(2,1)} %bitcast.13, bf16[512,128]{1,0:T(8,128)(2,1)} %bitcast.14, bf16[128,128]{1,0:T(8,128)(2,1)} %bitcast.15, ...), custom_call_target="tpu_custom_call" | custom-call | tf_op jit(solution)/shard_map/pallas_call | solution.py:409
  48.5 1.1 %shard_map.131 = (bf16[4096,128]{1,0:T(8,128)(2,1)}, f32[128,128]{1,0:T(8,128)}, f32[128,128]{1,0:T(8,128)}) custom-call(bf16[4096,128]{1,0:T(8,128)(2,1)S(1)} %get-tuple-element.9.o_ref, f32[128,128]{1,0:T(8,128)S(1)} %get-tuple-element.10.k_ref, f32[128,128]{1,0:T(8,128)S(1)} %get-tuple-element.11.v_ref), custom_call_target="tpu_custom_call" | custom-call | tf_op jit(solution)/shard_map/pallas_call | solution.py:438

commit v4 on v3

--- a/solution.py
+++ b/solution.py
@@ -30,10 +30,6 @@
     return lax.dot_general(a, b, (((1,), (0,)), ((), ())), preferred_element_type=f32)
 
 
-def dot_0(a, b):
-    return lax.dot_general(a, b, (((0,), (0,)), ((), ())), preferred_element_type=f32)
-
-
 def pick(x):
     x = x.reshape(TOKENS, 2, 8, 256)
     return jnp.concatenate([x[:, 0:1, :, :128], x[:, 1:2, :, 128:]], axis=1).reshape(R, 128)
@@ -44,7 +40,7 @@
     o_ref, gk_ref, gv_ref,
     tmp, kx, vx, dv, q_ref, g_ref, rk_ref, rv_ref, pk_ref, pv_ref, sk_ref, sv_ref,
     mask_ref, len_ref, cnt_ref, qe, ge, m1, l1, a1, e0, d0, wk, wv,
-    s1, s2, m2, gat, part, r1, r2, fin, acc_k, acc_v,
+    s1, s2, m2, gat, part, r1, r2, fin, acc, turned,
     in_sem, y_send, y_recv, x_send, x_recv, z_send, z_recv, s_send, s_recv,
     r1_send, r1_recv, r2_send, r2_recv, r3_send, r3_recv,
 ):
@@ -127,6 +123,7 @@
         q = q_ref[rows, :]
         q2 = jnp.concatenate([q * lo, q * hi], axis=1)
         qe[rows, :] = q2
+        turned[128:, rows] = q.T
         last = jnp.minimum(tok + i * TOKENS, length - 1)
         s = dot_t(q2, kx[pl.ds(0, 128 + nk), :])
         parts = [jnp.where((lane & 63) < count, s[:, :128], NEG)]
@@ -145,6 +142,7 @@
         g = (g_ref[rows, :].astype(f32) * live).astype(bf16)
         g2 = jnp.concatenate([g * lo, g * hi], axis=1)
         ge[rows, :] = g2
+        turned[:128, rows] = g.T
         m = m1[rows, :]
         cols = [jnp.exp2((s1[slot, :, pl.ds(j * 128, 128)] - m) * C) for j in range(1 + nk // 128)]
         p = jnp.concatenate(cols, axis=1)
@@ -299,8 +297,7 @@
     wk[pl.ds(512, 256), :] = rest(win[:, 32:40])
     wv[pl.ds(512, 256), :] = rest(win[:, 40:48])
 
-    acc_k[...] = jnp.zeros_like(acc_k)
-    acc_v[...] = jnp.zeros_like(acc_v)
+    acc[...] = jnp.zeros_like(acc)
 
     def prompt_scores(i, slot):
         rows = pl.ds(pl.multiple_of(i * R, R), R)
@@ -313,7 +310,7 @@
 
     def prompt_values(i, slot):
         rows = pl.ds(pl.multiple_of(i * R, R), R)
-        q2, g2 = qe[rows, :], ge[rows, :]
+        g2 = ge[rows, :]
         mo, m = m1[rows, :], m2[slot]
         cols = [jnp.exp2((s2[slot, :, pl.ds(j * 128, 128)] - m) * C) for j in range(6)]
         p = jnp.concatenate(cols, axis=1)
@@ -328,15 +325,15 @@
         inner = jnp.sum(g * mixed, axis=1, keepdims=True)
         ed = e0[rows, :] * (alpha * inv) * (d0[rows, :] - jnp.where(lane < 64, 0.0, inner))
         ed = ed.astype(bf16)
-        acc_v[...] += dot_0(ed, g2)[:64]
-        acc_k[...] += dot_0(ed, q2)[64:]
+        acc[...] += dot(turned[:, rows], jnp.concatenate([ed * lo, ed * hi], axis=1))
 
     staggered(prompt_scores, prompt_values, 0, CHUNKS)
 
-    part[pl.ds(0, 4)] = acc_k[:, :128].astype(bf16).reshape(4, 16, 128)
-    part[pl.ds(4, 4)] = acc_k[:, 128:].astype(bf16).reshape(4, 16, 128)
-    part[pl.ds(8, 4)] = acc_v[:, :128].astype(bf16).reshape(4, 16, 128)
-    part[pl.ds(12, 4)] = acc_v[:, 128:].astype(bf16).reshape(4, 16, 128)
+    sums = acc[...].T.astype(bf16)
+    part[pl.ds(0, 4)] = sums[64:128, 128:].reshape(4, 16, 128)
+    part[pl.ds(4, 4)] = sums[192:, 128:].reshape(4, 16, 128)
+    part[pl.ds(8, 4)] = sums[:64, :128].reshape(4, 16, 128)
+    part[pl.ds(12, 4)] = sums[128:192, :128].reshape(4, 16, 128)
 
     seat = resp * 2 + core
 
@@ -423,7 +420,7 @@
             vmem((2, R, 384), f32), vmem((2, R, 768), f32), vmem((2, R, 128), f32),
             vmem((128, 48, 128), bf16),
             vmem((16, 16, 128), bf16), vmem((16, 16, 128), bf16), vmem((8, 16, 128), bf16), vmem((16, 16, 128), bf16),
-            vmem((64, 256), f32), vmem((64, 256), f32),
+            vmem((256, 256), f32), vmem((256, ROWS), bf16),
             dma((11,)), dma((8, 2)), dma((8, 2)), dma((8, 4)), dma((8, 4)), dma((8, 4)), dma((8, 4)),
             dma((8,)), dma((8,)), dma((16,)), dma((16,)), dma((8,)), dma((8,)), dma((16,)), dma((16,)),
         ],

time: 49.8 us -> 49.5 us (level)
  no operation moved by 1% of the time
where the time goes in v4:
time: 49.5 us; the launch traced here: 49.3 us
  Pallas kernels  47.4 us (96%)
  between operations  1.93 us (4%)
    pallas_call x1, Pallas kernels, per_device(): pl.pallas_call(kernel, out_shape=[vmem((ROWS, 128), bf16), vmem((128, 128...  46.4 us
    pallas_call x1, Pallas kernels, per_device(): pl.pallas_call(place, out_shape=[jax.ShapeDtypeStruct((ROWS, 128), bf16),...  1.06 us

profile of v4, /device:TPU:1, one launch (start us, length us, event | category | flops | bytes accessed | tf_op | source)
XLA Modules:
  0.0 49.3 jit_solution(12722776252490195766)
XLA Ops:
  1.9 46.4 %shard_map.130 = (bf16[4096,128]{1,0:T(8,128)(2,1)S(1)}, f32[128,128]{1,0:T(8,128)S(1)}, f32[128,128]{1,0:T(8,128)S(1)}) custom-call(bf16[4096,128]{1,0:T(8,128)(2,1)} %bitcast.11, bf16[4096,128]{1,0:T(8,128)(2,1)} %bitcast.12, bf16[512,128]{1,0:T(8,128)(2,1)} %bitcast.13, bf16[512,128]{1,0:T(8,128)(2,1)} %bitcast.14, bf16[128,128]{1,0:T(8,128)(2,1)} %bitcast.15, ...), custom_call_target="tpu_custom_call" | custom-call | tf_op jit(solution)/shard_map/pallas_call | solution.py:406
  48.3 1.1 %shard_map.131 = (bf16[4096,128]{1,0:T(8,128)(2,1)}, f32[128,128]{1,0:T(8,128)}, f32[128,128]{1,0:T(8,128)}) custom-call(bf16[4096,128]{1,0:T(8,128)(2,1)S(1)} %get-tuple-element.9.o_ref, f32[128,128]{1,0:T(8,128)S(1)} %get-tuple-element.10.k_ref, f32[128,128]{1,0:T(8,128)S(1)} %get-tuple-element.11.v_ref), custom_call_target="tpu_custom_call" | custom-call | tf_op jit(solution)/shard_map/pallas_call | solution.py:435
